TPU v7x, 1024 devices: a whole 4x8x16 slice. The times are simulated.
1024 devices in a mesh: group: 32 (over y, x), slot: 32 (over z, core).
Axes of the slice: x: 4, y: 8, z: 16, core: 2. Of those that a mesh axis runs over, the one named last changes fastest.
Arguments:
- tokens: bfloat16 [131072, 2048], P(('group', 'slot')), may hold values from -6 to 6
- cotangent: bfloat16 [131072, 512], P(('group', 'slot')), may hold values from -0.59765625 to 0.59765625
- weight_halves: bfloat16 [1024, 1024, 512], P(('group', 'slot')), may hold values from -0.125 to 0.125
- momentum_halves: bfloat16 [1024, 1024, 512], P(('group', 'slot')), may hold values from -6 to 6
- old_map: int32 [32, 16], replicated, may hold values from 0 to 15, each once within a row
- new_map: int32 [32, 32], replicated, may hold values from 0 to 15, as said below
- row_ids: int32 [1024, 128], P(('group', 'slot')), may hold values from 0 to 127
Outputs:
- projected: bfloat16 [131072, 512], P(('group', 'slot'))
Inputs may be any that keep to these rules, and one draw needn't show every extreme that they name: `old_map`: each row names each of the group's experts once. `new_map`: every expert is hosted by one to four new slots; among the experts of every owner group one is hosted by exactly four.
All inputs are finite; a program needn't handle non-finite values.
Results may differ from a plain program's by a relative error of at most 0.007.
Values may be sent and summed in bfloat16 or wider, within the bound.
A program may use at most 32 MiB of HBM per device.

v0:
```python
import math

import jax
import jax.numpy as jnp
from jax import lax
from jax.sharding import PartitionSpec as P

ITERS = 2


coef_a = 3.4445
coef_b = -4.775
coef_c = 2.0315
momentum_rate = 0.95
step_scale = 0.01
gram_eps = 1e-06
contract_rows = (((0,), (0,)), ((), ()))


def swapped(shard, axis, stride):
    return lax.ppermute(shard, axis, [(i, i ^ 1 << stride) for i in range(lax.axis_size(axis))])


def pick_half(full_matrix, which_half, slot_count):
    row_count, col_count = full_matrix.shape
    pieces_view = full_matrix.reshape(slot_count, 2, row_count // (2 * slot_count), col_count)
    chosen = lax.dynamic_index_in_dim(pieces_view, which_half, axis=1, keepdims=False)
    return chosen.reshape(row_count // 2, col_count)


def inner_gram(half_rows):
    return lax.dot_general(
        half_rows, half_rows, contract_rows, preferred_element_type=jnp.float32
    ).astype(jnp.bfloat16)


def make_polynomial(scaled):
    gram_bf = scaled.astype(jnp.bfloat16)
    square = jnp.dot(gram_bf, gram_bf, preferred_element_type=jnp.float32)
    return (coef_b * scaled + coef_c * square).astype(jnp.bfloat16)


def on_device(tokens, cotangent, weight_halves, momentum_halves, old_map, new_map, row_ids):
    slot_count = lax.axis_size("slot")
    host_count = slot_count // lax.axis_size("group")
    model_width = tokens.shape[1]
    hidden = cotangent.shape[1]
    half_index = lax.axis_index("slot") % 2
    group_id = lax.axis_index("group")
    partial_value = lax.dot_general(
        tokens, cotangent, contract_rows, preferred_element_type=jnp.float32
    ).astype(jnp.bfloat16)
    received = swapped(pick_half(partial_value, 1 - half_index, slot_count), "slot", 0)
    gradient = pick_half(partial_value, half_index, slot_count).astype(
        jnp.float32
    ) + received.astype(jnp.float32)
    current = (momentum_rate * momentum_halves[0].astype(jnp.float32) + gradient).astype(
        jnp.bfloat16
    )
    own_gram = inner_gram(current)
    for iteration in range(ITERS):
        peer_gram = swapped(own_gram, "slot", 0)
        gram_sum = own_gram.astype(jnp.float32) + peer_gram.astype(jnp.float32)
        if iteration == 0:
            norm_sq = jnp.trace(gram_sum) + gram_eps
            gram_sum = gram_sum / norm_sq
            factor = 1.0 / jnp.sqrt(norm_sq)
        else:
            factor = 1.0
        polynomial = make_polynomial(gram_sum)
        product = jnp.dot(current, polynomial, preferred_element_type=jnp.float32)
        current = (factor * (coef_a * current.astype(jnp.float32) + product)).astype(jnp.bfloat16)
        if iteration + 1 < ITERS:
            own_gram = inner_gram(current)
    renewed = (
        weight_halves[0].astype(jnp.float32)
        - step_scale * math.sqrt(model_width) * current.astype(jnp.float32)
    ).astype(jnp.bfloat16)
    blocks = lax.all_to_all(
        renewed.reshape(slot_count, -1, hidden), "slot", split_axis=0, concat_axis=0, tiled=True
    )
    pieces = blocks.reshape(slot_count // 2, -1, hidden)
    requests = lax.dynamic_slice_in_dim(new_map, group_id * host_count, host_count, axis=1).reshape(
        -1
    )
    own_list = lax.dynamic_index_in_dim(old_map, group_id, 0, keepdims=False)
    holder = jnp.argmax((own_list[None, :] == requests[:, None]).astype(jnp.int32), axis=1)
    outgoing_blocks = jnp.take(pieces, holder, axis=0)
    weight_new = lax.all_to_all(
        lax.all_to_all(outgoing_blocks, "group", split_axis=0, concat_axis=0, tiled=True),
        "slot",
        split_axis=0,
        concat_axis=1,
        tiled=True,
    )[0]
    chosen = jnp.take(tokens, row_ids[0], axis=0)
    return jnp.dot(chosen, weight_new, preferred_element_type=jnp.float32).astype(jnp.bfloat16)


def solution(mesh):
    placed = (
        P(("group", "slot"), None),
        P(("group", "slot"), None),
        P(("group", "slot"), None, None),
        P(("group", "slot"), None, None),
        P(),
        P(),
        P(("group", "slot"), None),
    )
    return jax.shard_map(
        on_device, mesh=mesh, in_specs=placed, out_specs=P(("group", "slot"), None), check_vma=False
    )
```

profile of v0, /device:TPU:1, one launch (start us, length us, event | category | flops | bytes accessed | tf_op | source)
XLA Modules:
  0.0 271.7 jit_solution(15377455788226804398)
XLA Ops:
  0.0 1.0 copy-done
  1.0 1.6 convolution_convert_fusion
  2.9 16.2 %collective-permute-start = (bf16[1024,512]{1,0:T(8,128)(2,1)S(1)}, bf16[1024,512]{1,0:T(8,128)(2,1)S(1)}, u32[]{:S(2)}, u32[]{:S(2)}) collective-permute-start(bf16[1024,512]{1,0:T(8,128)(2,1)S(1)} %bitcast.31), channel_id=1, source_target_pairs={{0,1},{1,0},{2,3},{3,2},{4,5},{5,4},{6,7},{7,6},{8,9},{9,8},{10,11... | collective-permute-start | bytes 3145736 | tf_op jit(solution)/shard_map/ppermute | solution.py:21
  19.1 2.3 collective-permute-done
  21.4 0.5 fusion.1
  21.9 0.7 convolution_convert_fusion.2
  22.7 2.3 collective-permute-start.1
  25.0 1.5 collective-permute-done.1
  26.5 0.7 select_reduce_fusion
  27.8 2.1 multiply_convert_fusion
  30.0 2.4 convolution_convert_fusion.1
  32.3 2.3 collective-permute-start.2
  34.6 1.5 collective-permute-done.2
  36.1 3.8 %fusion.2 = bf16[1024,512]{1,0:T(8,128)(2,1)} fusion(bf16[1024,512]{1,0:T(8,128)(2,1)} %multiply_convert_fusion, bf16[1,1024,512]{2,1,0:T(8,128)(2,1)S(1)} %copy-done.4, bf16[512,512]{1,0:T(8,128)(2,1)S(1)} %collective-permute-done.2, bf16[512,512]{1,0:T(8,128)(2,1)S(1)} %convolution_convert_fusion.1), kind=kOutput, calls=%fused_computation.7 | convolution fusion | flops 812908544 | bytes 4194304 | tf_op jit(solution)/shard_map/dot_general | solution.py:71
  40.0 6.8 %all-to-all-start = ((bf16[32,32,512]{2,1,0:T(8,128)(2,1)}), bf16[32,32,512]{2,1,0:T(8,128)(2,1)S(1)}, u32[]{:S(2)}, u32[]{:S(2)}) async-start(bf16[32,32,512]{2,1,0:T(8,128)(2,1)} %bitcast.8), calls=%async_computation | async-start | bytes 2097152 | tf_op jit(solution)/shard_map/all_to_all | solution.py:79
  47.1 0.6 iota_reduce_fusion
  47.8 54.7 %all-to-all-done = bf16[32,32,512]{2,1,0:T(8,128)(2,1)S(1)} async-done(((bf16[32,32,512]{2,1,0:T(8,128)(2,1)}), bf16[32,32,512]{2,1,0:T(8,128)(2,1)S(1)}, u32[]{:S(2)}, u32[]{:S(2)}) %all-to-all-start) | async-done | bytes 1048608 | tf_op jit(solution)/shard_map/all_to_all | solution.py:79
  102.5 2.0 gather_fusion.1
  104.5 1.8 broadcast_select_fusion
  106.4 58.3 %all_to_all.19 = bf16[32,64,512]{2,1,0:T(8,128)(2,1)} all-to-all(bf16[32,64,512]{2,1,0:T(8,128)(2,1)S(1)} %broadcast_select_fusion), channel_id=1, replica_groups=mesh['group'=32,'slot'=32] {'group'}, dimensions={0} | all-to-all | bytes 4194304 | tf_op jit(solution)/shard_map/all_to_all | solution.py:90
  164.6 6.6 %all-to-all-start.2 = ((bf16[32,64,512]{2,1,0:T(8,128)(2,1)}), bf16[32,64,512]{2,1,0:T(8,128)(2,1)S(1)}, u32[]{:S(2)}, u32[]{:S(2)}) async-start(bf16[32,64,512]{2,1,0:T(8,128)(2,1)} %all_to_all.19), calls=%async_computation.2 | async-start | bytes 4194304 | tf_op jit(solution)/shard_map/all_to_all | solution.py:89
  171.2 0.9 gather_fusion
  172.2 98.3 %all-to-all-done.2 = bf16[32,64,512]{2,1,0:T(8,128)(2,1)S(1)} async-done(((bf16[32,64,512]{2,1,0:T(8,128)(2,1)}), bf16[32,64,512]{2,1,0:T(8,128)(2,1)S(1)}, u32[]{:S(2)}, u32[]{:S(2)}) %all-to-all-start.2) | async-done | bytes 2097184 | tf_op jit(solution)/shard_map/all_to_all | solution.py:89
  270.5 1.1 convolution_convert_fusion.3
  (20 shorter events, 0.7 us)
Async XLA Ops:
  0.0 1.0 copy-start
  2.7 18.7 %copy-start.1 = (bf16[1,1024,512]{2,1,0:T(8,128)(2,1)S(1)}, bf16[1,1024,512]{2,1,0:T(8,128)(2,1)}, u32[]{:S(2)}) copy-start(bf16[1,1024,512]{2,1,0:T(8,128)(2,1)} %param.10) | copy-start | bytes 3145732
  2.9 18.5 %collective-permute-start = (bf16[1024,512]{1,0:T(8,128)(2,1)S(1)}, bf16[1024,512]{1,0:T(8,128)(2,1)S(1)}, u32[]{:S(2)}, u32[]{:S(2)}) collective-permute-start(bf16[1024,512]{1,0:T(8,128)(2,1)S(1)} %bitcast.31), channel_id=1, source_target_pairs={{0,1},{1,0},{2,3},{3,2},{4,5},{5,4},{6,7},{7,6},{8,9},{9,8},{10,11... | collective-permute-start | bytes 3145736 | tf_op jit(solution)/shard_map/ppermute | solution.py:21
  22.7 3.8 %collective-permute-start.1 = (bf16[512,512]{1,0:T(8,128)(2,1)S(1)}, bf16[512,512]{1,0:T(8,128)(2,1)S(1)}, u32[]{:S(2)}, u32[]{:S(2)}) collective-permute-start(bf16[512,512]{1,0:T(8,128)(2,1)S(1)} %convolution_convert_fusion.2), channel_id=1, source_target_pairs={{0,1},{1,0},{2,3},{3,2},{4,5},{5,4},{6,7},{7,6},{8,9},{9,8},{10,11... | collective-permute-start | bytes 1572872 | tf_op jit(solution)/shard_map/ppermute | solution.py:21
  30.0 6.2 %copy-start.4 = (bf16[1,1024,512]{2,1,0:T(8,128)(2,1)S(1)}, bf16[1,1024,512]{2,1,0:T(8,128)(2,1)}, u32[]{:S(2)}) copy-start(bf16[1,1024,512]{2,1,0:T(8,128)(2,1)} %param.9) | copy-start | bytes 3145732
  32.3 3.8 %collective-permute-start.2 = (bf16[512,512]{1,0:T(8,128)(2,1)S(1)}, bf16[512,512]{1,0:T(8,128)(2,1)S(1)}, u32[]{:S(2)}, u32[]{:S(2)}) collective-permute-start(bf16[512,512]{1,0:T(8,128)(2,1)S(1)} %convolution_convert_fusion.1), channel_id=1, source_target_pairs={{0,1},{1,0},{2,3},{3,2},{4,5},{5,4},{6,7},{7,6},{8,9},{9,8},{10,11... | collective-permute-start | bytes 1572872 | tf_op jit(solution)/shard_map/ppermute | solution.py:21
  40.0 6.8 %copy-start.3 = (s32[32,16]{0,1:T(8,128)S(1)}, s32[32,16]{0,1:T(8,128)}, u32[]{:S(2)}) copy-start(s32[32,16]{0,1:T(8,128)} %param.11) | copy-start | bytes 6148
  40.0 7.0 %copy-start.2 = (s32[32,32]{1,0:T(8,128)S(1)}, s32[32,32]{1,0:T(8,128)}, u32[]{:S(2)}) copy-start(s32[32,32]{1,0:T(8,128)} %param.12) | copy-start | bytes 12292
  40.0 62.5 %all-to-all-start = ((bf16[32,32,512]{2,1,0:T(8,128)(2,1)}), bf16[32,32,512]{2,1,0:T(8,128)(2,1)S(1)}, u32[]{:S(2)}, u32[]{:S(2)}) async-start(bf16[32,32,512]{2,1,0:T(8,128)(2,1)} %bitcast.8), calls=%async_computation | async-start | bytes 2097152 | tf_op jit(solution)/shard_map/all_to_all | solution.py:79
  164.6 6.6 %copy-start.5 = (s32[1,128]{1,0:T(1,128)S(1)}, s32[1,128]{1,0:T(1,128)}, u32[]{:S(2)}) copy-start(s32[1,128]{1,0:T(1,128)} %param.13) | copy-start | bytes 1540
  164.6 105.9 %all-to-all-start.2 = ((bf16[32,64,512]{2,1,0:T(8,128)(2,1)}), bf16[32,64,512]{2,1,0:T(8,128)(2,1)S(1)}, u32[]{:S(2)}, u32[]{:S(2)}) async-start(bf16[32,64,512]{2,1,0:T(8,128)(2,1)} %all_to_all.19), calls=%async_computation.2 | async-start | bytes 4194304 | tf_op jit(solution)/shard_map/all_to_all | solution.py:89
where the time goes:
time: 274 us; the launch traced here: 272 us
  waiting for transfers between devices  158 us (58%)
  blocking collectives  58.3 us (21%)
  starting transfers between devices  34.1 us (12%)
  matrix products  11.8 us (4%)
  local copies, waits for them, and re-layouts  4.64 us (2%)
  other arithmetic  3.66 us (1%)
    all_to_all x1, waiting for transfers between devices, on_device(): lax.all_to_all(lax.all_to_all(outgoing_blocks, 'group', split_axis=0, con...  98.3 us
    all_to_all x1, blocking collectives, on_device(): lax.all_to_all(outgoing_blocks, 'group', split_axis=0, concat_axis=0, til...  58.3 us
    all_to_all x1, waiting for transfers between devices, on_device(): lax.all_to_all(renewed.reshape(slot_count, -1, hidden), 'slot', split_axi...  54.7 us
    ppermute x3, starting transfers between devices, swapped(): lax.ppermute(shard, axis, [(i, i ^ 1 << stride) for i in range(lax.axis_s...  20.8 us
    all_to_all x1, starting transfers between devices, on_device(): lax.all_to_all(renewed.reshape(slot_count, -1, hidden), 'slot', split_axi...  6.77 us
    all_to_all x1, starting transfers between devices, on_device(): lax.all_to_all(lax.all_to_all(outgoing_blocks, 'group', split_axis=0, con...  6.58 us
    dot_general x2, matrix products, on_device(): product = jnp.dot(current, polynomial, preferred_element_type=jnp.float32)  5.97 us
  transfers between devices with their start and end apart: 5, of which 5 were waited for; matrix products, arithmetic and copies ran while one was open for 1% of the time, Pallas kernels for 0%

commit v1 on v0

v1 whole, which is shorter than its diff:
```python
import functools
import math

import jax
import jax.numpy as jnp
from jax import lax
from jax.experimental import pallas as pl
from jax.experimental.pallas import tpu as pltpu
from jax.sharding import PartitionSpec as P

ITERS = 2
CAP = 4
BLK = 32
SUB = 2
MESH = pl.DeviceIdType.MESH
BF16, F32 = jnp.bfloat16, jnp.float32
VMEM = pltpu.VMEM
DMA = pltpu.SemaphoreType.DMA

coef_a = 3.4445
coef_b = -4.775
coef_c = 2.0315
momentum_rate = 0.95
step_scale = 0.01
gram_eps = 1e-06
ROWS = (((0,), (0,)), ((), ()))


def dot(a, b):
    return jnp.dot(a, b, preferred_element_type=F32)


def dot_rows(a, b):
    return lax.dot_general(a, b, ROWS, preferred_element_type=F32)


def loop(count, body):
    lax.fori_loop(0, count, lambda i, c: (body(i), c)[1], 0)


def kernel(
    groups, slots,
    table, tokens, cot, rows, weight_hbm, moment_hbm,
    out,
    weight, moment, halves, picked, got_parts, sent, landed, result, spread, back, answer, final,
    own_part, send_part, peer_part, x, gram, gram_peer, total, poly, full,
    load_sem, p_send, p_recv, f_send, f_recv, a_send, a_recv, r_send, r_recv, b_send, b_recv,
    g_send, g_recv, m_send, m_recv, w_send, w_recv,
):
    g, s = lax.axis_index("group"), lax.axis_index("slot")
    h = lax.rem(s, 2)
    mate = (g, s + 1 - 2 * h)
    n_rows, width = tokens.shape
    hidden = cot.shape[1]
    half = width // 2
    diagonal = g == s

    barrier = pltpu.get_barrier_semaphore()

    def hello(device):
        pl.semaphore_signal(barrier, inc=1, device_id=device, device_id_type=MESH)

    loop(groups - 1, lambda i: hello((lax.rem(g + 1 + i, groups), s)))
    loop(slots - 1, lambda i: hello((g, lax.rem(s + 1 + i, slots))))

    def hello_sender(i):
        c = lax.rem(s + i, groups)

        @pl.when(jnp.logical_not(jnp.logical_and(diagonal, c == g)))
        def _():
            hello((c, g))

    loop(groups, hello_sender)

    load_w = pltpu.make_async_copy(weight_hbm.at[0], weight, load_sem.at[0])
    load_m = pltpu.make_async_copy(moment_hbm.at[0], moment, load_sem.at[1])
    load_w.start()
    load_m.start()

    wide = 8 * BLK
    col = lax.broadcasted_iota(jnp.int32, (wide, wide), 1)
    row = lax.broadcasted_iota(jnp.int32, (wide, wide), 0)
    inner = col % (wide // 2)
    origin = (inner // BLK) * (2 * BLK) + (col // (wide // 2)) * BLK + inner % BLK
    order = (row == origin).astype(F32).astype(BF16)
    pick = (lax.broadcasted_iota(jnp.int32, (n_rows, n_rows), 0) == rows[...]).astype(F32).astype(BF16)
    for b in range(width // wide):
        sorted_cols = dot(tokens[:, b * wide : (b + 1) * wide], order).astype(BF16)
        chosen = dot_rows(pick, sorted_cols).astype(BF16)
        for k in range(2):
            where = slice(b * wide // 2, (b + 1) * wide // 2)
            piece = slice(k * wide // 2, (k + 1) * wide // 2)
            halves[k, :, where] = sorted_cols[:, piece]
            picked[:, k * half + where.start : k * half + where.stop] = chosen[:, piece]

    tall = n_rows // SUB
    high = tall // 16
    across = groups // high
    cw = width // across

    def piece_of(q, c):
        return picked.at[
            pl.ds(pl.multiple_of(q * tall + (c // across) * 16, 16), 16),
            pl.ds(pl.multiple_of(lax.rem(c, across) * cw, cw), cw),
        ]

    @pl.when(diagonal)
    def _():
        pl.semaphore_wait(barrier, groups - 1 + slots - 1 + slots - 1)

    @pl.when(jnp.logical_not(diagonal))
    def _():
        pl.semaphore_wait(barrier, groups - 1 + slots - 1 + slots)

    for q in range(SUB):

        def send_piece(i, q=q):
            c = lax.rem(g + 1 + i, groups)
            pltpu.make_async_remote_copy(
                piece_of(q, c), got_parts[q].at[g], p_send, p_recv.at[q], device_id=(c, s), device_id_type=MESH
            ).start()

        loop(groups - 1, send_piece)
        pltpu.make_async_copy(piece_of(q, g), got_parts[q].at[g], p_recv.at[q]).start()

    parts = 2
    tile = half // parts
    grads = []
    for part in range(parts):
        where = pl.ds(part * tile, tile)
        send_part[where, :] = dot_rows(halves[1 - h, :, part * tile : (part + 1) * tile], cot[...]).astype(BF16)
        copy = pltpu.make_async_remote_copy(
            send_part.at[where], peer_part.at[where], g_send.at[part], g_recv.at[part],
            device_id=mate, device_id_type=MESH,
        )
        copy.start()
        grads.append(copy)
    for part in range(parts):
        own_part[pl.ds(part * tile, tile), :] = dot_rows(
            halves[h, :, part * tile : (part + 1) * tile], cot[...]
        ).astype(BF16)

    def forward(k, q):
        def select(t):
            sent[k, q, t] = got_parts[q][table[(t // 2) * CAP + 2 * k + lax.rem(t, 2)]]

        loop(slots, select)
        place = landed.at[
            k,
            pl.ds(pl.multiple_of(q * tall + (g // across) * 16, 16), 16),
            pl.ds(pl.multiple_of(lax.rem(g, across) * cw, cw), cw),
        ]

        def send(i):
            t = lax.rem(s + 1 + i, slots)
            itself = jnp.logical_and(diagonal, t == s)

            @pl.when(jnp.logical_not(itself))
            def _():
                pltpu.make_async_remote_copy(
                    sent.at[k, q, t], place, f_send, f_recv.at[k], device_id=(s, t), device_id_type=MESH
                ).start()

            @pl.when(itself)
            def _():
                pltpu.make_async_copy(sent.at[k, q, t], place, f_recv.at[k]).start()

        loop(slots, send)

    def wait_pieces(q):
        pltpu.make_async_copy(got_parts[q], got_parts[q], p_recv.at[q]).wait()

    for q in range(SUB):
        wait_pieces(q)
        forward(0, q)
    for q in range(SUB):
        forward(1, q)

    chunk = 256

    def share_gram(t):
        total[...] = jnp.zeros_like(total)

        def add(i):
            block = x[pl.ds(pl.multiple_of(i * chunk, chunk), chunk), :]
            total[...] += dot_rows(block, block)

        loop(half // chunk, add)
        gram[t] = total[...].astype(BF16)
        copy = pltpu.make_async_remote_copy(
            gram.at[t], gram_peer.at[t], m_send.at[t], m_recv.at[t], device_id=mate, device_id_type=MESH
        )
        copy.start()
        return copy

    load_m.wait()
    for copy in grads:
        copy.wait_recv()

    def first(i):
        where = pl.ds(pl.multiple_of(i * chunk, chunk), chunk)
        grad = own_part[where, :].astype(F32) + peer_part[where, :].astype(F32)
        x[where, :] = (momentum_rate * moment[where, :].astype(F32) + grad).astype(BF16)

    loop(half // chunk, first)
    grams = []
    factor = None
    for t in range(ITERS):
        copy = share_gram(t)
        copy.wait_recv()
        grams.append(copy)
        both = gram[t].astype(F32) + gram_peer[t].astype(F32)
        if t == 0:
            on_diagonal = lax.broadcasted_iota(jnp.int32, both.shape, 0) == lax.broadcasted_iota(
                jnp.int32, both.shape, 1
            )
            norm_sq = jnp.sum(jnp.where(on_diagonal, both, 0.0), axis=(0, 1), keepdims=True) + gram_eps
            both = both / norm_sq
            factor = 1.0 / jnp.sqrt(norm_sq)
        total[...] = both
        gram_bf = both.astype(BF16)
        poly[...] = (coef_b * total[...] + coef_c * dot(gram_bf, gram_bf)).astype(BF16)
        if t + 1 == ITERS:
            load_w.wait()

        def step(i, t=t, factor=factor):
            where = pl.ds(pl.multiple_of(i * chunk, chunk), chunk)
            block = x[where, :]
            new = coef_a * block.astype(F32) + dot(block, poly[...])
            if t == 0:
                new = factor * new
            new = new.astype(BF16)
            if t + 1 < ITERS:
                x[where, :] = new
            else:
                full[h, where, :] = (
                    weight[where, :].astype(F32) - step_scale * math.sqrt(width) * new.astype(F32)
                ).astype(BF16)

        loop(half // chunk, step)
    whole = pltpu.make_async_remote_copy(
        full.at[h], full.at[h], w_send, w_recv, device_id=mate, device_id_type=MESH
    )
    whole.start()
    whole.wait_recv()

    out_high = n_rows // 16
    out_across = groups // out_high
    ow = hidden // out_across

    def tile_of(ref, c):
        return ref.at[
            pl.ds(pl.multiple_of((c // out_across) * 16, 16), 16),
            pl.ds(pl.multiple_of(lax.rem(c, out_across) * ow, ow), ow),
        ]

    for k in range(2):
        pltpu.make_async_copy(landed.at[k], landed.at[k], f_recv.at[k]).wait()
        product = dot(landed[k, :, :half], full[0]) + dot(landed[k, :, half:], full[1])
        result[k] = product.astype(BF16)

        def spread_out(i, k=k):
            c = lax.rem(g + 1 + i, groups)
            pltpu.make_async_remote_copy(
                tile_of(result.at[k], c), spread.at[k, g], a_send, a_recv.at[k, g],
                device_id=(c, s), device_id_type=MESH,
            ).start()

        loop(groups - 1, spread_out)
        pltpu.make_async_copy(tile_of(result.at[k], g), spread.at[k, g], a_recv.at[k, g]).start()

        def pass_on(i, k=k):
            o = lax.rem(g + lax.rem(i, 2) * groups + (1 - 2 * lax.rem(i, 2)) * ((i + 1) // 2), groups)
            pltpu.make_async_copy(spread.at[k, o], spread.at[k, o], a_recv.at[k, o]).wait()

            @pl.when(o != s)
            def _():
                pltpu.make_async_remote_copy(
                    spread.at[k, o], back.at[k * slots + s], r_send, r_recv.at[k],
                    device_id=(g, o), device_id_type=MESH,
                ).start()

            @pl.when(o == s)
            def _():
                pltpu.make_async_copy(spread.at[k, o], back.at[k * slots + s], r_recv.at[k]).start()

        loop(groups, pass_on)

    for k in range(2):
        these = back.at[pl.ds(k * slots, slots)]
        pltpu.make_async_copy(these, these, r_recv.at[k]).wait()

    def answer_one(c):
        answer[c] = back[table[slots * 2 + c]]

    loop(groups, answer_one)

    def give(i):
        c = lax.rem(g + 1 + i, groups)
        pltpu.make_async_remote_copy(
            answer.at[c], tile_of(final, g), b_send, b_recv, device_id=(c, s), device_id_type=MESH
        ).start()

    loop(groups - 1, give)
    pltpu.make_async_copy(answer.at[g], tile_of(final, g), b_recv).start()

    def left(ref, sem):
        pltpu.make_async_copy(ref, ref, sem).wait()

    for copy in grads + grams + [whole]:
        copy.wait_send()
    for q in range(SUB):
        left(got_parts[q].at[pl.ds(0, groups - 1)], p_send)
    for k in range(2):
        left(spread.at[k, pl.ds(0, groups - 1)], a_send)
        left(back.at[pl.ds(0, slots - 1)], r_send)
        for q in range(SUB):
            left(sent.at[k, q, pl.ds(0, slots - 1)], f_send)

            @pl.when(jnp.logical_not(diagonal))
            def _():
                left(sent.at[k, q, 0], f_send)

    left(answer.at[pl.ds(0, groups - 1)], b_send)
    pltpu.make_async_copy(final, final, b_recv).wait()
    out[...] = final[...]


def on_device(tokens, cotangent, weight_halves, momentum_halves, old_map, new_map, row_ids):
    slots, groups = lax.axis_size("slot"), lax.axis_size("group")
    n_rows, width = tokens.shape
    hidden = cotangent.shape[1]
    half = width // 2
    experts = slots // 2

    owner = lax.axis_index("slot")
    held = lax.dynamic_index_in_dim(old_map, owner, 0, keepdims=False)
    asked = lax.dynamic_index_in_dim(new_map, owner, 1, keepdims=False)
    one = jnp.arange(groups, dtype=jnp.int32)
    hit = (held[None, :] == asked[:, None]).astype(jnp.int32)
    holder = jnp.sum(hit * jnp.arange(experts, dtype=jnp.int32)[None, :], axis=1)
    earlier = (asked[None, :] == asked[:, None]) & (one[None, :] < one[:, None])
    rank = jnp.sum(earlier.astype(jnp.int32), axis=1)
    place = holder * CAP + rank
    mine = place[None, :] == jnp.arange(experts * CAP, dtype=jnp.int32)[:, None]
    source = jnp.sum(mine.astype(jnp.int32) * one[None, :], axis=1)
    origin = (rank // 2) * slots + holder * 2 + rank % 2
    table = jnp.concatenate([source, origin])

    tall = n_rows // SUB
    cw = width // (groups // (tall // 16))
    ow = hidden // (groups // (n_rows // 16))
    vm = pl.BlockSpec(memory_space=VMEM)
    hbm = pl.BlockSpec(memory_space=pl.ANY)
    return pl.pallas_call(
        functools.partial(kernel, groups, slots),
        out_shape=jax.ShapeDtypeStruct((n_rows, hidden), BF16),
        in_specs=[pl.BlockSpec(memory_space=pltpu.SMEM), vm, vm, vm, hbm, hbm],
        out_specs=vm,
        scratch_shapes=[
            VMEM((half, hidden), BF16),
            VMEM((half, hidden), BF16),
            VMEM((2, n_rows, half), BF16),
            VMEM((n_rows, width), BF16),
            [VMEM((groups, 16, cw), BF16)] * SUB,
            VMEM((2, SUB, slots, 16, cw), BF16),
            VMEM((2, n_rows, width), BF16),
            VMEM((2, n_rows, hidden), BF16),
            VMEM((2, groups, 16, ow), BF16),
            VMEM((2 * slots, 16, ow), BF16),
            VMEM((groups, 16, ow), BF16),
            VMEM((n_rows, hidden), BF16),
            VMEM((half, hidden), BF16),
            VMEM((half, hidden), BF16),
            VMEM((half, hidden), BF16),
            VMEM((half, hidden), BF16),
            VMEM((ITERS, hidden, hidden), BF16),
            VMEM((ITERS, hidden, hidden), BF16),
            VMEM((hidden, hidden), F32),
            VMEM((hidden, hidden), BF16),
            VMEM((2, half, hidden), BF16),
            DMA((2,)),
            DMA,
            DMA((SUB,)),
            DMA,
            DMA((2,)),
            DMA,
            DMA((2, groups)),
            DMA,
            DMA((2,)),
            DMA,
            DMA,
            DMA((2,)),
            DMA((2,)),
            DMA((ITERS,)),
            DMA((ITERS,)),
            DMA,
            DMA,
        ],
        compiler_params=pltpu.CompilerParams(
            collective_id=0, has_side_effects=True, vmem_limit_bytes=48 << 20
        ),
        name="muon_route",
    )(table, tokens, cotangent, row_ids, weight_halves, momentum_halves)


def solution(mesh):
    placed = (
        P(("group", "slot"), None),
        P(("group", "slot"), None),
        P(("group", "slot"), None, None),
        P(("group", "slot"), None, None),
        P(),
        P(),
        P(("group", "slot"), None),
    )
    return jax.shard_map(
        on_device, mesh=mesh, in_specs=placed, out_specs=P(("group", "slot"), None), check_vma=False
    )
```

time: 274 us -> 124 us (0.45)
  waiting for transfers between devices: 158 us -> 0 us
  Pallas kernels: 0 us -> 116 us
  blocking collectives: 58.3 us -> 0 us
  starting transfers between devices: 34.1 us -> 0 us
  matrix products: 11.8 us -> 0 us
  other arithmetic: 3.66 us -> 0.45 us
    all_to_all x2 -> x0, waiting for transfers between devices: 153 us -> none  [the longest x1 98.3 us: on_device(): lax.all_to_all(lax.all_to_all(outgoing_blocks, 'group', split_axis=0, con...]
    pallas_call x0 -> x1, Pallas kernels: none -> 116 us  [on_device(): pl.pallas_call(functools.partial(kernel, groups, slots), out_shape=jax.Sh...]
    all_to_all x1 -> x0, blocking collectives: 58.3 us -> none  [on_device(): lax.all_to_all(outgoing_blocks, 'group', split_axis=0, concat_axis=0, til...]
    ppermute x3 -> x0, starting transfers between devices: 20.8 us -> none  [swapped(): lax.ppermute(shard, axis, [(i, i ^ 1 << stride) for i in range(lax.axis_s...]
    all_to_all x2 -> x0, starting transfers between devices: 13.4 us -> none  [the longest x1 6.77 us: on_device(): lax.all_to_all(renewed.reshape(slot_count, -1, hidden), 'slot', split_axi...]
    dot_general x6 -> x0, matrix products: 11.8 us -> none  [the longest x2 5.97 us: on_device(): product = jnp.dot(current, polynomial, preferred_element_type=jnp.float32)]
    unnamed x12 -> x15, local copies, waits for them, and re-layouts: 1.06 us -> 6.86 us
    ppermute x3 -> x0, waiting for transfers between devices: 5.3 us -> none  [swapped(): lax.ppermute(shard, axis, [(i, i ^ 1 << stride) for i in range(lax.axis_s...]
  transfers between devices with their start and end apart: 5 -> 0, of which waited for: 5 -> 0; matrix products, arithmetic and copies ran while one was open for 1% -> 0% of each run, Pallas kernels for 0% -> 0%
where the time goes in v1:
time: 124 us
  Pallas kernels  116 us (94%)
  local copies, waits for them, and re-layouts  7.22 us (6%)
    pallas_call x1, Pallas kernels, on_device(): pl.pallas_call(functools.partial(kernel, groups, slots), out_shape=jax.Sh...  116 us
    unnamed x15, local copies, waits for them, and re-layouts  6.86 us

profile of v1, /device:TPU:1, one launch (start us, length us, event | category | flops | bytes accessed | tf_op | source)
XLA Modules:
  0.0 123.8 jit_solution(10576930021433950120)
XLA Ops:
  0.0 0.0 copy-start
  0.0 0.7 copy-done
  0.7 0.0 copy-start.6
  0.7 0.2 dynamic-slice_reduce_fusion
  0.9 0.5 copy-done.6
  1.4 0.2 dynamic-slice_reduce_fusion.1
  1.6 0.1 select_reduce_fusion.1
  1.7 0.2 convert_reduce_fusion
  1.9 0.1 select_reduce_fusion
  2.0 0.0 copy-start.5
  2.0 0.1 pad_add_fusion.table
  2.1 0.6 copy-done.5
  2.6 0.0 copy-start.1
  2.6 1.2 copy-done.1
  3.9 0.0 copy-start.2
  3.9 1.2 copy-done.2
  5.1 0.0 copy-start.3
  5.1 1.0 copy-done.3
  6.1 0.0 copy-start.4
  6.1 0.9 copy-done.4
  7.0 116.0 %muon_route.1 = bf16[128,512]{1,0:T(8,128)(2,1)S(1)} custom-call(s32[96]{0:T(128)S(1)} %pad_add_fusion.table, bf16[128,2048]{1,0:T(8,128)(2,1)S(1)} %copy-done.3, bf16[128,512]{1,0:T(8,128)(2,1)S(1)} %copy-done.4, s32[1,128]{1,0:T(1,128)S(1)} %copy-done.5, bf16[1,1024,512]{2,1,0:T(8,128)(2,1)S(1)} %copy-done.1, bf16[1,1024,512]{2,1,0:T(8,128)(2,1)S(1)} %copy-done.2), custom_call_target="tpu_custom_call" | custom-call | tf_op jit(solution)/shard_map/muon_route/pallas_call | solution.py:355
  123.1 0.7 copy.9
  (1 shorter events, 0.0 us)
Async XLA Ops:
  0.0 0.7 copy-start
  0.7 0.7 copy-start.6
  2.0 0.7 copy-start.5
  2.6 1.2 copy-start.1
  3.9 1.2 copy-start.2
  5.1 1.0 copy-start.3
  6.1 0.9 copy-start.4

commit v2 on v1

--- a/solution.py
+++ b/solution.py
@@ -11,7 +11,7 @@
 ITERS = 2
 CAP = 4
 BLK = 32
-SUB = 2
+SUB = 4
 MESH = pl.DeviceIdType.MESH
 BF16, F32 = jnp.bfloat16, jnp.float32
 VMEM = pltpu.VMEM
@@ -40,9 +40,9 @@
 
 def kernel(
     groups, slots,
-    table, tokens, cot, rows, weight_hbm, moment_hbm,
+    old_map, new_map, rows, tokens_hbm, cot_hbm, weight_hbm, moment_hbm,
     out,
-    weight, moment, halves, picked, got_parts, sent, landed, result, spread, back, answer, final,
+    tokens, cot, weight, moment, halves, table_rows, table, got_parts, sent, landed, result, spread, back, answer, final,
     own_part, send_part, peer_part, x, gram, gram_peer, total, poly, full,
     load_sem, p_send, p_recv, f_send, f_recv, a_send, a_recv, r_send, r_recv, b_send, b_recv,
     g_send, g_recv, m_send, m_recv, w_send, w_recv,
@@ -55,6 +55,20 @@
     half = width // 2
     diagonal = g == s
 
+    loads = [
+        pltpu.make_async_copy(source, target, load_sem.at[n])
+        for n, (source, target) in enumerate(
+            (
+                (tokens_hbm, tokens),
+                (cot_hbm, cot),
+                (moment_hbm.at[0], moment),
+                (weight_hbm.at[0], weight),
+            )
+        )
+    ]
+    for load in loads:
+        load.start()
+
     barrier = pltpu.get_barrier_semaphore()
 
     def hello(device):
@@ -71,27 +85,6 @@
             hello((c, g))
 
     loop(groups, hello_sender)
-
-    load_w = pltpu.make_async_copy(weight_hbm.at[0], weight, load_sem.at[0])
-    load_m = pltpu.make_async_copy(moment_hbm.at[0], moment, load_sem.at[1])
-    load_w.start()
-    load_m.start()
-
-    wide = 8 * BLK
-    col = lax.broadcasted_iota(jnp.int32, (wide, wide), 1)
-    row = lax.broadcasted_iota(jnp.int32, (wide, wide), 0)
-    inner = col % (wide // 2)
-    origin = (inner // BLK) * (2 * BLK) + (col // (wide // 2)) * BLK + inner % BLK
-    order = (row == origin).astype(F32).astype(BF16)
-    pick = (lax.broadcasted_iota(jnp.int32, (n_rows, n_rows), 0) == rows[...]).astype(F32).astype(BF16)
-    for b in range(width // wide):
-        sorted_cols = dot(tokens[:, b * wide : (b + 1) * wide], order).astype(BF16)
-        chosen = dot_rows(pick, sorted_cols).astype(BF16)
-        for k in range(2):
-            where = slice(b * wide // 2, (b + 1) * wide // 2)
-            piece = slice(k * wide // 2, (k + 1) * wide // 2)
-            halves[k, :, where] = sorted_cols[:, piece]
-            picked[:, k * half + where.start : k * half + where.stop] = chosen[:, piece]
 
     tall = n_rows // SUB
     high = tall // 16
@@ -99,7 +92,7 @@
     cw = width // across
 
     def piece_of(q, c):
-        return picked.at[
+        return tokens.at[
             pl.ds(pl.multiple_of(q * tall + (c // across) * 16, 16), 16),
             pl.ds(pl.multiple_of(lax.rem(c, across) * cw, cw), cw),
         ]
@@ -112,6 +105,7 @@
     def _():
         pl.semaphore_wait(barrier, groups - 1 + slots - 1 + slots)
 
+    loads[0].wait()
     for q in range(SUB):
 
         def send_piece(i, q=q):
@@ -122,6 +116,44 @@
 
         loop(groups - 1, send_piece)
         pltpu.make_async_copy(piece_of(q, g), got_parts[q].at[g], p_recv.at[q]).start()
+
+    experts = slots // 2
+
+    def iota(shape, axis):
+        return lax.broadcasted_iota(jnp.int32, shape, axis)
+
+    def total_of(mask, value, axis):
+        return jnp.sum(jnp.where(mask, value, 0), axis=axis, keepdims=True)
+
+    square = (groups, groups)
+    asked = total_of(iota((groups, slots), 1) == s, new_map[...], 1)
+    asked_row = total_of(iota(square, 0) == iota(square, 1), asked, 0)
+    held = total_of(iota((experts, groups), 1) == s, old_map[...], 1)
+    held = total_of(iota((experts, experts), 0) == iota((experts, experts), 1), held, 0)
+    holder = total_of(asked == held, iota((groups, experts), 1), 1)
+    earlier = jnp.logical_and(asked == asked_row, iota(square, 1) < iota(square, 0))
+    rank = total_of(earlier, jnp.ones(square, jnp.int32), 1)
+    rank_half = (rank >= 2).astype(jnp.int32)
+    source = total_of(holder * CAP + rank == iota((groups, experts * CAP), 1), iota((groups, experts * CAP), 0), 0)
+    table_rows[...] = jnp.zeros_like(table_rows)
+    table_rows[0:1, 0 : experts * CAP] = jnp.minimum(source, groups - 1)
+    origin = jnp.minimum(rank_half * slots + holder * 2 + rank - 2 * rank_half, 2 * slots - 1)
+    table_rows[1:2, 0:groups] = total_of(iota(square, 0) == iota(square, 1), origin, 0)
+    to_scalars = pltpu.make_async_copy(table_rows, table, load_sem.at[4])
+    to_scalars.start()
+
+    wide = 8 * BLK
+    col = iota((wide, wide), 1)
+    inner = col % (wide // 2)
+    came_from = (inner // BLK) * (2 * BLK) + (col // (wide // 2)) * BLK + inner % BLK
+    order = (iota((wide, wide), 0) == came_from).astype(F32).astype(BF16)
+    for b in range(width // wide):
+        sorted_cols = dot(tokens[:, b * wide : (b + 1) * wide], order).astype(BF16)
+        for k in range(2):
+            halves[k, :, b * wide // 2 : (b + 1) * wide // 2] = sorted_cols[
+                :, k * wide // 2 : (k + 1) * wide // 2
+            ]
+    loads[1].wait()
 
     parts = 2
     tile = half // parts
@@ -140,11 +172,13 @@
             halves[h, :, part * tile : (part + 1) * tile], cot[...]
         ).astype(BF16)
 
-    def forward(k, q):
-        def select(t):
-            sent[k, q, t] = got_parts[q][table[(t // 2) * CAP + 2 * k + lax.rem(t, 2)]]
-
-        loop(slots, select)
+    def forward(rank_of, q):
+        k, core = rank_of // 2, rank_of % 2
+
+        def select(p):
+            sent[k, q, 2 * p + core] = got_parts[q][table[0, p * CAP + rank_of]]
+
+        loop(experts, select)
         place = landed.at[
             k,
             pl.ds(pl.multiple_of(q * tall + (g // across) * 16, 16), 16),
@@ -152,7 +186,7 @@
         ]
 
         def send(i):
-            t = lax.rem(s + 1 + i, slots)
+            t = 2 * lax.rem(s // 2 + 1 + i, experts) + core
             itself = jnp.logical_and(diagonal, t == s)
 
             @pl.when(jnp.logical_not(itself))
@@ -165,16 +199,18 @@
             def _():
                 pltpu.make_async_copy(sent.at[k, q, t], place, f_recv.at[k]).start()
 
-        loop(slots, send)
+        loop(experts, send)
 
     def wait_pieces(q):
         pltpu.make_async_copy(got_parts[q], got_parts[q], p_recv.at[q]).wait()
 
+    to_scalars.wait()
     for q in range(SUB):
         wait_pieces(q)
         forward(0, q)
-    for q in range(SUB):
-        forward(1, q)
+    for rank_of in range(1, CAP):
+        for q in range(SUB):
+            forward(rank_of, q)
 
     chunk = 256
 
@@ -193,7 +229,7 @@
         copy.start()
         return copy
 
-    load_m.wait()
+    loads[2].wait()
     for copy in grads:
         copy.wait_recv()
 
@@ -221,7 +257,7 @@
         gram_bf = both.astype(BF16)
         poly[...] = (coef_b * total[...] + coef_c * dot(gram_bf, gram_bf)).astype(BF16)
         if t + 1 == ITERS:
-            load_w.wait()
+            loads[3].wait()
 
         def step(i, t=t, factor=factor):
             where = pl.ds(pl.multiple_of(i * chunk, chunk), chunk)
@@ -233,13 +269,14 @@
             if t + 1 < ITERS:
                 x[where, :] = new
             else:
-                full[h, where, :] = (
-                    weight[where, :].astype(F32) - step_scale * math.sqrt(width) * new.astype(F32)
-                ).astype(BF16)
+                renewed = weight[where, :].astype(F32) - step_scale * math.sqrt(width) * new.astype(F32)
+                full[pl.ds(i * (chunk // BLK), chunk // BLK), h] = renewed.astype(BF16).reshape(
+                    chunk // BLK, BLK, hidden
+                )
 
         loop(half // chunk, step)
     whole = pltpu.make_async_remote_copy(
-        full.at[h], full.at[h], w_send, w_recv, device_id=mate, device_id_type=MESH
+        full.at[:, h], full.at[:, h], w_send, w_recv, device_id=mate, device_id_type=MESH
     )
     whole.start()
     whole.wait_recv()
@@ -256,8 +293,7 @@
 
     for k in range(2):
         pltpu.make_async_copy(landed.at[k], landed.at[k], f_recv.at[k]).wait()
-        product = dot(landed[k, :, :half], full[0]) + dot(landed[k, :, half:], full[1])
-        result[k] = product.astype(BF16)
+        result[k] = dot(landed[k], full[...].reshape(width, hidden)).astype(BF16)
 
         def spread_out(i, k=k):
             c = lax.rem(g + 1 + i, groups)
@@ -291,7 +327,7 @@
         pltpu.make_async_copy(these, these, r_recv.at[k]).wait()
 
     def answer_one(c):
-        answer[c] = back[table[slots * 2 + c]]
+        answer[c] = back[table[1, c]]
 
     loop(groups, answer_one)
 
@@ -323,7 +359,8 @@
 
     left(answer.at[pl.ds(0, groups - 1)], b_send)
     pltpu.make_async_copy(final, final, b_recv).wait()
-    out[...] = final[...]
+    pick = (iota((n_rows, n_rows), 0) == rows[...]).astype(F32).astype(BF16)
+    out[...] = dot_rows(pick, final[...]).astype(BF16)
 
 
 def on_device(tokens, cotangent, weight_halves, momentum_halves, old_map, new_map, row_ids):
@@ -331,22 +368,6 @@
     n_rows, width = tokens.shape
     hidden = cotangent.shape[1]
     half = width // 2
-    experts = slots // 2
-
-    owner = lax.axis_index("slot")
-    held = lax.dynamic_index_in_dim(old_map, owner, 0, keepdims=False)
-    asked = lax.dynamic_index_in_dim(new_map, owner, 1, keepdims=False)
-    one = jnp.arange(groups, dtype=jnp.int32)
-    hit = (held[None, :] == asked[:, None]).astype(jnp.int32)
-    holder = jnp.sum(hit * jnp.arange(experts, dtype=jnp.int32)[None, :], axis=1)
-    earlier = (asked[None, :] == asked[:, None]) & (one[None, :] < one[:, None])
-    rank = jnp.sum(earlier.astype(jnp.int32), axis=1)
-    place = holder * CAP + rank
-    mine = place[None, :] == jnp.arange(experts * CAP, dtype=jnp.int32)[:, None]
-    source = jnp.sum(mine.astype(jnp.int32) * one[None, :], axis=1)
-    origin = (rank // 2) * slots + holder * 2 + rank % 2
-    table = jnp.concatenate([source, origin])
-
     tall = n_rows // SUB
     cw = width // (groups // (tall // 16))
     ow = hidden // (groups // (n_rows // 16))
@@ -355,13 +376,16 @@
     return pl.pallas_call(
         functools.partial(kernel, groups, slots),
         out_shape=jax.ShapeDtypeStruct((n_rows, hidden), BF16),
-        in_specs=[pl.BlockSpec(memory_space=pltpu.SMEM), vm, vm, vm, hbm, hbm],
+        in_specs=[vm, vm, vm, hbm, hbm, hbm, hbm],
         out_specs=vm,
         scratch_shapes=[
+            VMEM((n_rows, width), BF16),
+            VMEM((n_rows, hidden), BF16),
             VMEM((half, hidden), BF16),
             VMEM((half, hidden), BF16),
             VMEM((2, n_rows, half), BF16),
-            VMEM((n_rows, width), BF16),
+            VMEM((8, 128), jnp.int32),
+            pltpu.SMEM((8, 128), jnp.int32),
             [VMEM((groups, 16, cw), BF16)] * SUB,
             VMEM((2, SUB, slots, 16, cw), BF16),
             VMEM((2, n_rows, width), BF16),
@@ -378,8 +402,8 @@
             VMEM((ITERS, hidden, hidden), BF16),
             VMEM((hidden, hidden), F32),
             VMEM((hidden, hidden), BF16),
-            VMEM((2, half, hidden), BF16),
-            DMA((2,)),
+            VMEM((half // BLK, 2, BLK, hidden), BF16),
+            DMA((5,)),
             DMA,
             DMA((SUB,)),
             DMA,
@@ -398,10 +422,10 @@
             DMA,
         ],
         compiler_params=pltpu.CompilerParams(
-            collective_id=0, has_side_effects=True, vmem_limit_bytes=48 << 20
+            collective_id=0, has_side_effects=True, vmem_limit_bytes=60 << 20
         ),
         name="muon_route",
-    )(table, tokens, cotangent, row_ids, weight_halves, momentum_halves)
+    )(old_map.T, new_map, row_ids, tokens, cotangent, weight_halves, momentum_halves)
 
 
 def solution(mesh):

time: 124 us -> 115 us (0.927)
  local copies, waits for them, and re-layouts: 7.22 us -> 1.57 us
  Pallas kernels: 116 us -> 113 us
    unnamed x15 -> x1, local copies, waits for them, and re-layouts: 6.86 us -> 1.57 us
    pallas_call x1, Pallas kernels: 116 us -> 113 us  [on_device(): pl.pallas_call(functools.partial(kernel, groups, slots), out_shape=jax.Sh...]
where the time goes in v2:
time: 115 us
  Pallas kernels  113 us (98%)
  local copies, waits for them, and re-layouts  1.57 us (1%)
    pallas_call x1, Pallas kernels, on_device(): pl.pallas_call(functools.partial(kernel, groups, slots), out_shape=jax.Sh...  113 us

profile of v2, /device:TPU:1, one launch (start us, length us, event | category | flops | bytes accessed | tf_op | source)
XLA Modules:
  0.0 114.6 jit_solution(764243678537820848)
XLA Ops:
  0.0 113.0 %muon_route.1 = bf16[128,512]{1,0:T(8,128)(2,1)} custom-call(s32[16,32]{1,0:T(8,128)} %bitcast.1, s32[32,32]{1,0:T(8,128)} %new_map.1, s32[1,128]{1,0:T(1,128)} %rows.1, bf16[128,2048]{1,0:T(8,128)(2,1)} %tokens_hbm.1, bf16[128,512]{1,0:T(8,128)(2,1)} %cot_hbm.1, bf16[1,1024,512]{2,1,0:T(8,128)(2,1)} %weight_hbm.1, bf16[1,1024,512]{2,1,0:T(8,128)(2,1)} %moment_hbm.1), custom_call_target="tpu_custom_call" | custom-call | tf_op jit(solution)/shard_map/muon_route/pallas_call | solution.py:376
  113.0 1.6 %copy.9 = bf16[128,512]{1,0:T(8,128)(2,1)} copy(bf16[128,512]{1,0:T(8,128)(2,1)} %muon_route.1) | data formatting | bytes 262144

commit v3 on v2

--- a/solution.py
+++ b/solution.py
@@ -142,6 +142,46 @@
     to_scalars = pltpu.make_async_copy(table_rows, table, load_sem.at[4])
     to_scalars.start()
 
+    def forward(rank_of, q):
+        k, core = rank_of // 2, rank_of % 2
+
+        def select(p):
+            sent[k, q, 2 * p + core] = got_parts[q][table[0, p * CAP + rank_of]]
+
+        loop(experts, select)
+        place = landed.at[
+            k,
+            pl.ds(pl.multiple_of(q * tall + (g // across) * 16, 16), 16),
+            pl.ds(pl.multiple_of(lax.rem(g, across) * cw, cw), cw),
+        ]
+
+        def send(i):
+            t = 2 * lax.rem(s // 2 + 1 + i, experts) + core
+            itself = jnp.logical_and(diagonal, t == s)
+
+            @pl.when(jnp.logical_not(itself))
+            def _():
+                pltpu.make_async_remote_copy(
+                    sent.at[k, q, t], place, f_send, f_recv.at[k], device_id=(s, t), device_id_type=MESH
+                ).start()
+
+            @pl.when(itself)
+            def _():
+                pltpu.make_async_copy(sent.at[k, q, t], place, f_recv.at[k]).start()
+
+        loop(experts, send)
+
+    def wait_pieces(q):
+        pltpu.make_async_copy(got_parts[q], got_parts[q], p_recv.at[q]).wait()
+
+    to_scalars.wait()
+    for q in range(SUB):
+        wait_pieces(q)
+        forward(0, q)
+    for rank_of in range(1, CAP):
+        for q in range(SUB):
+            forward(rank_of, q)
+
     wide = 8 * BLK
     col = iota((wide, wide), 1)
     inner = col % (wide // 2)
@@ -171,46 +211,6 @@
         own_part[pl.ds(part * tile, tile), :] = dot_rows(
             halves[h, :, part * tile : (part + 1) * tile], cot[...]
         ).astype(BF16)
-
-    def forward(rank_of, q):
-        k, core = rank_of // 2, rank_of % 2
-
-        def select(p):
-            sent[k, q, 2 * p + core] = got_parts[q][table[0, p * CAP + rank_of]]
-
-        loop(experts, select)
-        place = landed.at[
-            k,
-            pl.ds(pl.multiple_of(q * tall + (g // across) * 16, 16), 16),
-            pl.ds(pl.multiple_of(lax.rem(g, across) * cw, cw), cw),
-        ]
-
-        def send(i):
-            t = 2 * lax.rem(s // 2 + 1 + i, experts) + core
-            itself = jnp.logical_and(diagonal, t == s)
-
-            @pl.when(jnp.logical_not(itself))
-            def _():
-                pltpu.make_async_remote_copy(
-                    sent.at[k, q, t], place, f_send, f_recv.at[k], device_id=(s, t), device_id_type=MESH
-                ).start()
-
-            @pl.when(itself)
-            def _():
-                pltpu.make_async_copy(sent.at[k, q, t], place, f_recv.at[k]).start()
-
-        loop(experts, send)
-
-    def wait_pieces(q):
-        pltpu.make_async_copy(got_parts[q], got_parts[q], p_recv.at[q]).wait()
-
-    to_scalars.wait()
-    for q in range(SUB):
-        wait_pieces(q)
-        forward(0, q)
-    for rank_of in range(1, CAP):
-        for q in range(SUB):
-            forward(rank_of, q)
 
     chunk = 256
 

time: 115 us -> 114 us (level)
  no operation moved by 1% of the time
where the time goes in v3:
time: 114 us; the launch traced here: 113 us
  Pallas kernels  112 us (98%)
  local copies, waits for them, and re-layouts  1.57 us (1%)
    pallas_call x1, Pallas kernels, on_device(): pl.pallas_call(functools.partial(kernel, groups, slots), out_shape=jax.Sh...  112 us

profile of v3, /device:TPU:1, one launch (start us, length us, event | category | flops | bytes accessed | tf_op | source)
XLA Modules:
  0.0 113.4 jit_solution(14824745814089845181)
XLA Ops:
  0.0 111.8 %muon_route.1 = bf16[128,512]{1,0:T(8,128)(2,1)} custom-call(s32[16,32]{1,0:T(8,128)} %bitcast.1, s32[32,32]{1,0:T(8,128)} %new_map.1, s32[1,128]{1,0:T(1,128)} %rows.1, bf16[128,2048]{1,0:T(8,128)(2,1)} %tokens_hbm.1, bf16[128,512]{1,0:T(8,128)(2,1)} %cot_hbm.1, bf16[1,1024,512]{2,1,0:T(8,128)(2,1)} %weight_hbm.1, bf16[1,1024,512]{2,1,0:T(8,128)(2,1)} %moment_hbm.1), custom_call_target="tpu_custom_call" | custom-call | tf_op jit(solution)/shard_map/muon_route/pallas_call | solution.py:376
  111.9 1.6 %copy.9 = bf16[128,512]{1,0:T(8,128)(2,1)} copy(bf16[128,512]{1,0:T(8,128)(2,1)} %muon_route.1) | data formatting | bytes 262144
